TPU v7x, 512 devices: a whole 4x8x8 slice. The times are simulated.
512 devices in a mesh: lon: 64 (over z, x, core), lat: 8 (over y).
Axes of the slice: x: 4, y: 8, z: 8, core: 2. Of those that a mesh axis runs over, the one named last changes fastest.
Arguments:
- spec_pts: bfloat16 [36, 36, 262144], P(None, None, ('lon', 'lat')), may hold values from 0.049804688 to 2
- wind_u: float32 [262144], P(('lon', 'lat')), may hold values from -40 to 40
- wind_v: float32 [262144], P(('lon', 'lat')), may hold values from -40 to 40
- ocean_current: bfloat16 [2, 8, 512, 128], P(None, 'lat', 'lon'), may hold values from -0.099609375 to 0.099609375
- block_owner: int32 [32, 64], P('lat', 'lon'), may hold values from 0 to 63, as said below
- block_slot: int32 [32, 64], P('lat', 'lon'), may hold values from 0 to 7, as said below
- cell_source: int32 [32, 8192], P('lat', 'lon'), may hold values from 0 to 511, as said below
- land_mask: int32 [32, 8192], P('lat', 'lon'), may hold values 0 or 1
Outputs:
- spectrum_out: bfloat16 [36, 36, 32, 8192], P(None, None, 'lat', 'lon')
Inputs may be any that keep to these rules, and one draw needn't show every extreme that they name: Within each band of 4 grid rows, the pairs (block_owner, block_slot) over all its rows and tile columns are distinct, each owner's slots run from 0 to its count of blocks minus one; an owner holds between 0 and 8 blocks, and at least one owner holds exactly 8. `block_slot`: see block_owner. `cell_source`: within each tile of 4 x 128 cells, the values are a permutation of 0 to 511.
All inputs are finite; a program needn't handle non-finite values. No bound on the sum of `land_mask` on one device may be relied on, other than what follows from the above.
Results may differ from a plain program's by a relative error of at most 0.001.
The roundings to bfloat16 on the way count: a program that leaves them out, or rounds other values in their place, can miss the bound.
Values may be sent and summed in bfloat16 or wider, within the bound.
A program may use at most 128 MiB of HBM per device.

v0:
```python
import jax
import jax.numpy as jnp
from jax import lax
from jax.sharding import PartitionSpec as P

fastest = 0.53
turn_scale = 2.5


def with_halo(shard, sides, width, wrap):
    for axis, dim in sides:
        devices, length = (lax.axis_size(axis), shard.shape[dim])
        up = [(i, (i + 1) % devices) for i in range(devices if wrap else devices - 1)]
        down = [(j, i) for i, j in up]
        last = lax.slice_in_dim(shard, length - width, length, axis=dim)
        leading = lax.slice_in_dim(shard, 0, width, axis=dim)
        before = lax.ppermute(last, axis, up)
        after = lax.ppermute(leading, axis, down)
        shard = jnp.concatenate([before, shard, after], axis=dim)
    return shard


def tables(freqs, dirs):
    ratio = 1.1 ** jnp.arange(freqs).astype(jnp.float32)
    group_speed = fastest / ratio
    phase_speed = 44.6 / ratio
    relative = ratio / ratio[freqs - 1]
    spacing = 2.0 * jnp.pi / dirs
    theta = (jnp.arange(dirs).astype(jnp.float32) + 0.5) * spacing
    facing = (jnp.arange(dirs).astype(jnp.float32) + 1.0) * spacing
    return (
        group_speed,
        phase_speed,
        relative,
        jnp.cos(theta),
        jnp.sin(theta),
        jnp.cos(facing),
        jnp.sin(facing),
    )


def grow(energy, proj, phase_val, rel_val, mean_energy):
    drive = jnp.maximum(proj / phase_val - 1.0, 0.0)
    gain = 0.5 * jnp.tanh(0.2 * drive)
    loss = 0.3 * rel_val * (mean_energy / 0.5) ** 2
    return (energy * jnp.exp(gain - loss)).astype(jnp.bfloat16)


def turning(ux, uy, vx, vy, face_cos, face_sin):
    return turn_scale * (
        face_sin * face_cos * (ux - vy) + face_sin * face_sin * uy - face_cos * face_cos * vx
    )


def body(spec_pts, wind_u, wind_v, ocean_current, block_owner, block_slot, cell_source, land_mask):
    freqs, dirs, points = spec_pts.shape
    lat_rows, lon_cells = cell_source.shape
    n_lon = lax.axis_size("lon")
    n_lat = lax.axis_size("lat")
    per_dest = points // (n_lon * n_lat)
    capacity = ocean_current.shape[2]
    spectral = freqs * dirs
    group_speed, phase_speed, relative, cosd, sind, face_cos, face_sin = tables(freqs, dirs)
    wanted = block_owner[:, 0] * capacity + block_slot[:, 0]
    piece = lax.all_gather(ocean_current, "lon", axis=2, tiled=True)
    count = piece.shape[2]
    inside = (wanted >= 0) & (wanted < count)
    taken = jnp.take(piece[:, 0], jnp.clip(wanted, 0, count - 1), axis=1)
    currents = jnp.where(
        inside[None, :, None], taken, jnp.zeros((2, lat_rows, lon_cells), jnp.bfloat16)
    )
    mean_energy = jnp.sum(spec_pts.astype(jnp.float32), axis=(0, 1)) / (freqs * dirs)
    proj = wind_u[None, :] * cosd[:, None] + wind_v[None, :] * sind[:, None]
    sourced = grow(
        spec_pts.astype(jnp.float32),
        proj[None],
        phase_speed[:, None, None],
        relative[:, None, None],
        mean_energy[None, None, :],
    )
    packed = sourced.reshape(spectral, points).T.reshape(n_lat, n_lon, per_dest, spectral)
    section = lax.all_to_all(packed, "lat", split_axis=0, concat_axis=0, tiled=True)
    moved_in = lax.all_to_all(section, "lon", split_axis=1, concat_axis=1, tiled=True)
    regrouped = moved_in.reshape(points, spectral)
    sea_bf = land_mask.astype(jnp.bfloat16)
    picked = jnp.take(regrouped, cell_source.reshape(-1), axis=0).reshape(
        lat_rows, lon_cells, spectral
    )
    tile = picked.transpose(0, 2, 1) * sea_bf[:, None, :]
    extras = jnp.stack([currents[0], currents[1], sea_bf], axis=1)
    wide_tile, wide_extra = (
        with_halo(tile, (("lon", 2),), 1, True),
        with_halo(extras, (("lon", 2),), 1, True),
    )
    tall_tile, tall_extra = (
        with_halo(tile, (("lat", 0),), 1, False),
        with_halo(extras, (("lat", 0),), 1, False),
    )
    energy = tile.astype(jnp.float32).reshape(lat_rows, freqs, dirs, lon_cells)
    wide = wide_tile.astype(jnp.float32).reshape(lat_rows, freqs, dirs, lon_cells + 2)
    tall = tall_tile.astype(jnp.float32).reshape(lat_rows + 2, freqs, dirs, lon_cells)
    wide_aux = wide_extra.astype(jnp.float32)
    tall_aux = tall_extra.astype(jnp.float32)
    speed_grid = group_speed[None, :, None, None]
    wide_u, wide_v, wide_sea = (wide_aux[:, 0], wide_aux[:, 1], wide_aux[:, 2])
    open_x = wide_sea[:, :-1] * wide_sea[:, 1:]
    face_u = 0.5 * (wide_u[:, :-1] + wide_u[:, 1:])
    cx = speed_grid * cosd[None, None, :, None] + face_u[:, None, None, :]
    flux_x = open_x[:, None, None, :] * (
        jnp.maximum(cx, 0.0) * wide[..., :-1] + jnp.minimum(cx, 0.0) * wide[..., 1:]
    )
    div_x = flux_x[..., 1:] - flux_x[..., :-1]
    tall_u, tall_v, tall_sea = (tall_aux[:, 0], tall_aux[:, 1], tall_aux[:, 2])
    open_y = tall_sea[:-1] * tall_sea[1:]
    face_v = 0.5 * (tall_v[:-1] + tall_v[1:])
    cy = speed_grid * sind[None, None, :, None] + face_v[:, None, None, :]
    flux_y = open_y[:, None, None, :] * (
        jnp.maximum(cy, 0.0) * tall[:-1] + jnp.minimum(cy, 0.0) * tall[1:]
    )
    div_y = flux_y[1:] - flux_y[:-1]
    moved = energy - div_x - div_y
    ux = 0.5 * (wide_u[:, 2:] - wide_u[:, :-2])
    vx = 0.5 * (wide_v[:, 2:] - wide_v[:, :-2])
    uy = 0.5 * (tall_u[2:] - tall_u[:-2])
    vy = 0.5 * (tall_v[2:] - tall_v[:-2])
    turn = turning(
        ux[:, None, :],
        uy[:, None, :],
        vx[:, None, :],
        vy[:, None, :],
        face_cos[None, :, None],
        face_sin[None, :, None],
    )
    turn_grid = turn[:, None]
    upper = jnp.roll(moved, -1, axis=2)
    flux_turn = jnp.maximum(turn_grid, 0.0) * moved + jnp.minimum(turn_grid, 0.0) * upper
    turned = moved - (flux_turn - jnp.roll(flux_turn, 1, axis=2))
    sea = land_mask.astype(jnp.float32)
    result = (turned * sea[:, None, None, :]).astype(jnp.bfloat16)
    return result.transpose(1, 2, 0, 3)


def solution(mesh):
    return jax.shard_map(
        body,
        mesh=mesh,
        in_specs=(
            P(None, None, ("lon", "lat")),
            P(("lon", "lat")),
            P(("lon", "lat")),
            P(None, "lat", "lon", None),
            P("lat", "lon"),
            P("lat", "lon"),
            P("lat", "lon"),
            P("lat", "lon"),
        ),
        out_specs=P(None, None, "lat", "lon"),
        check_vma=False,
    )
```

profile of v0, /device:TPU:1, one launch (start us, length us, event | category | flops | bytes accessed | tf_op | source)
XLA Modules:
  0.0 206.6 jit_solution(12400354524479043120)
XLA Ops:
  0.1 1.7 convert_reduce_fusion
  1.8 0.6 slice.155
  2.3 0.7 divide_multiply_fusion
  3.0 0.1 broadcast_multiply_fusion
  3.1 0.8 multiply_add_fusion
  3.9 2.6 %fusion.14 = bf16[36,36,512]{2,1,0:T(8,128)(2,1)S(1)} fusion(bf16[36,36,512]{2,1,0:T(8,128)(2,1)} %param.8, f32[36,512]{1,0:T(8,128)S(1)} %broadcast_multiply_fusion, f32[36]{0:T(128)S(1)} %fusion.41, f32[36,512]{1,0:T(8,128)S(1)} %multiply_add_fusion), kind=kLoop, calls=%fused_computation.23 | loop fusion | flops 5971968 | bytes 2801808 | tf_op jit(solution)/shard_map/convert_element_type | solution.py:46
  6.5 0.3 reshape.362
  6.8 0.0 copy-start.3
  6.8 0.0 copy-start.5
  6.8 0.0 copy-start.4
  6.8 1.6 copy.68
  8.4 7.7 %all-to-all-start = ((bf16[8,64,1,1296]{3,1,2,0:T(8,128)(2,1)}), bf16[8,64,1,1296]{3,1,2,0:T(8,128)(2,1)S(1)}, u32[]{:S(2)}, u32[]{:S(2)}) async-start(bf16[8,64,1,1296]{3,1,2,0:T(8,128)(2,1)} %bitcast.2), calls=%async_computation | async-start | bytes 2883584 | tf_op jit(solution)/shard_map/all_to_all | solution.py:82
  16.1 51.1 %all_gather.3 = bf16[2,1,512,128]{3,0,1,2:T(2,128)(2,1)S(1)} all-gather(bf16[2,1,8,128]{3,0,1,2:T(2,128)(2,1)S(1)} %copy.74), channel_id=1, replica_groups=mesh['lon'=64,'lat'=8] {'lon'}, dimensions={2}, use_global_device_ids=true | all-gather | bytes 266240 | tf_op jit(solution)/shard_map/all_gather | solution.py:65
  67.2 0.6 gather_fusion.1
  67.8 0.1 fusion.37
  67.9 1.3 collective-permute-start.5
  69.2 4.3 %collective-permute-start.4 = (bf16[1,3,128]{2,0,1:T(2,128)(2,1)S(1)}, bf16[1,3,128]{2,0,1:T(2,128)(2,1)S(1)}, u32[]{:S(2)}, u32[]{:S(2)}) collective-permute-start(bf16[1,3,128]{2,0,1:T(2,128)(2,1)S(1)} %get-tuple-element.22), channel_id=1, source_target_pairs={{0,1},{1,2},{2,3},{3,4},{4,5},{5,6},{6,7},{8,9},{9,10},{10,11},{11... | collective-permute-start | bytes 2312 | tf_op jit(solution)/shard_map/ppermute | solution.py:17
  73.5 0.1 fusion.50
  73.6 2.4 %collective-permute-start.1 = (bf16[4,3,1]{2,0,1:T(4,128)(2,1)S(1)}, bf16[4,3,1]{2,0,1:T(4,128)(2,1)S(1)}, u32[]{:S(2)}, u32[]{:S(2)}) collective-permute-start(bf16[4,3,1]{2,0,1:T(4,128)(2,1)S(1)} %get-tuple-element.21), channel_id=1, source_target_pairs={{8,0},{16,8},{24,16},{32,24},{40,32},{48,40},{56,48},{64,56},{72,6... | collective-permute-start | bytes 80 | tf_op jit(solution)/shard_map/ppermute | solution.py:18
  75.9 3.2 %collective-permute-start = (bf16[4,3,1]{2,0,1:T(4,128)(2,1)S(1)}, bf16[4,3,1]{2,0,1:T(4,128)(2,1)S(1)}, u32[]{:S(2)}, u32[]{:S(2)}) collective-permute-start(bf16[4,3,1]{2,0,1:T(4,128)(2,1)S(1)} %get-tuple-element.20), channel_id=1, source_target_pairs={{0,8},{8,16},{16,24},{24,32},{32,40},{40,48},{48,56},{56,64},{64,7... | collective-permute-start | bytes 80 | tf_op jit(solution)/shard_map/ppermute | solution.py:17
  79.2 1.9 copy.69
  81.2 7.9 %all-to-all-start.1 = ((bf16[8,64,1,1296]{3,0,2,1:T(8,128)(2,1)}), bf16[8,64,1,1296]{3,0,2,1:T(8,128)(2,1)S(1)}, u32[]{:S(2)}, u32[]{:S(2)}) async-start(bf16[8,64,1,1296]{3,0,2,1:T(8,128)(2,1)} %copy.69), calls=%async_computation.1 | async-start | bytes 2883584 | tf_op jit(solution)/shard_map/all_to_all | solution.py:83
  89.2 0.1 copy.72
  89.3 0.1 copy.67
  89.5 0.1 broadcast_multiply_fusion.2
  89.6 0.1 maximum_convert_fusion.2
  89.7 0.1 fusion.29
  89.7 0.1 slice_multiply_fusion.1
  89.8 0.1 fusion.30
  89.9 0.1 fusion.35
  90.0 0.8 fusion.25
  90.8 34.7 %all-to-all-done.1 = bf16[8,64,1,1296]{3,0,2,1:T(8,128)(2,1)S(1)} async-done(((bf16[8,64,1,1296]{3,0,2,1:T(8,128)(2,1)}), bf16[8,64,1,1296]{3,0,2,1:T(8,128)(2,1)S(1)}, u32[]{:S(2)}, u32[]{:S(2)}) %all-to-all-start.1) | async-done | bytes 1327136 | tf_op jit(solution)/shard_map/all_to_all | solution.py:83
  125.5 0.1 copy.70
  125.7 2.1 %gather_fusion = bf16[512,1296]{1,0:T(8,128)(2,1)S(1)} fusion(bf16[512,1296]{1,0:T(8,128)(2,1)S(1)} %bitcast.48, s32[1024]{0:T(1024)S(1)} %pad_clamp_fusion.1), kind=kCustom, calls=%fused_computation | custom fusion | bytes 2656256 | tf_op jit(solution)/shard_map/jit(_take)/gather | solution.py:86
  127.8 2.2 %fusion.22 = bf16[4,1296,128]{1,0,2:T(4,128)(2,1)S(1)} fusion(bf16[4,128,1296]{2,1,0:T(8,128)(2,1)S(1)} %bitcast.55, pred[4,128]{0,1:T(8,128)(4,1)S(1)} %copy.67, bf16[4,128]{0,1:T(8,128)(2,1)S(1)} %copy.72), kind=kLoop, calls=%fused_computation.38 | loop fusion | flops 1327104 | bytes 2655744 | tf_op jit(solution)/shard_map/mul | solution.py:89
  130.0 0.6 fusion.48
  130.6 3.3 %collective-permute-start.3 = (bf16[4,1296,1]{1,0,2:T(4,128)(2,1)}, bf16[4,1296,1]{1,0,2:T(4,128)(2,1)}, u32[]{:S(2)}, u32[]{:S(2)}) collective-permute-start(bf16[4,1296,1]{1,0,2:T(4,128)(2,1)} %get-tuple-element.10), channel_id=1, source_target_pairs={{8,0},{16,8},{24,16},{32,24},{40,32},{48,40},{56,48},{64,56},{72,6... | collective-permute-start | bytes 31112 | tf_op jit(solution)/shard_map/ppermute | solution.py:18
  133.9 3.0 %collective-permute-start.2 = (bf16[4,1296,1]{1,0,2:T(4,128)(2,1)}, bf16[4,1296,1]{1,0,2:T(4,128)(2,1)}, u32[]{:S(2)}, u32[]{:S(2)}) collective-permute-start(bf16[4,1296,1]{1,0,2:T(4,128)(2,1)} %get-tuple-element.9), channel_id=1, source_target_pairs={{0,8},{8,16},{16,24},{24,32},{32,40},{40,48},{48,56},{56,64},{64,7... | collective-permute-start | bytes 31112 | tf_op jit(solution)/shard_map/ppermute | solution.py:17
  136.9 1.9 fusion.49
  138.8 2.0 copy.73
  140.8 2.8 %copy.78 = bf16[1,1296,128]{2,1,0:T(8,128)(2,1)} copy(bf16[1,1296,128]{1,0,2:T(2,128)(2,1)} %get-tuple-element.12) | data formatting | bytes 663552 | tf_op jit(solution)/shard_map/slice | solution.py:16
  143.6 1.3 collective-permute-start.7
  144.9 1.7 copy.77
  146.6 4.7 %collective-permute-start.6 = (bf16[1,1296,128]{2,1,0:T(8,128)(2,1)}, bf16[1,1296,128]{2,1,0:T(8,128)(2,1)}, u32[]{:S(2)}, u32[]{:S(2)}) collective-permute-start(bf16[1,1296,128]{2,1,0:T(8,128)(2,1)} %copy.77), channel_id=1, source_target_pairs={{0,1},{1,2},{2,3},{3,4},{4,5},{5,6},{6,7},{8,9},{9,10},{10,11},{11... | collective-permute-start | bytes 995336 | tf_op jit(solution)/shard_map/ppermute | solution.py:17
  151.4 0.8 concatenate.27
  152.2 2.6 %copy.76 = bf16[4,36,36,1]{3,0,2,1:T(4,128)(2,1)} copy(bf16[4,36,36,1]{2,1,0,3:T(8,128)(2,1)S(1)} %concatenate.27) | data formatting | bytes 20736 | tf_op jit(solution)/shard_map/concatenate | solution.py:19
  154.8 0.8 concatenate.26
  155.6 2.6 %copy.75 = bf16[4,36,36,1]{3,0,2,1:T(4,128)(2,1)} copy(bf16[4,36,36,1]{2,1,0,3:T(8,128)(2,1)S(1)} %concatenate.26) | data formatting | bytes 20736 | tf_op jit(solution)/shard_map/concatenate | solution.py:19
  158.2 4.8 %maximum_convert_fusion.1 = f32[4,36,36,130]{3,0,2,1:T(4,128)S(1)} fusion(bf16[4,36,36,1]{3,0,2,1:T(4,128)(2,1)} %copy.76, bf16[4,36,36,128]{3,0,2,1:T(4,128)(2,1)S(1)} %bitcast.53, bf16[4,36,36,1]{3,0,2,1:T(4,128)(2,1)} %copy.75), kind=kLoop, calls=%fused_computation.29 | loop fusion | flops 4043520 | bytes 4043520 | tf_op jit(solution)/shard_map/convert_element_type | solution.py:100
  163.0 5.6 %fusion.2 = f32[4,36,36,129]{3,0,2,1:T(4,128)} fusion(f32[4,36,36,130]{3,0,2,1:T(4,128)S(1)} %maximum_convert_fusion.1, f32[4,129]{1,0:T(4,128)S(1)} %fusion.29, f32[36,36]{1,0:T(8,128)S(1)} %get-tuple-element.29, f32[4,129]{1,0:T(4,128)S(1)} %slice_multiply_fusion.1), kind=kLoop, calls=%fused_computation.8 | loop fusion | flops 4681152 | bytes 8034144 | tf_op jit(solution)/shard_map/mul | solution.py:109
  168.6 2.3 %copy.80 = bf16[1,1296,128]{1,0,2:T(2,128)(2,1)S(1)} copy(bf16[1,1296,128]{2,1,0:T(8,128)(2,1)} %collective-permute-done.7) | data formatting | bytes 663552 | tf_op jit(solution)/shard_map/ppermute | solution.py:18
  170.9 2.9 %copy.79 = bf16[1,1296,128]{1,0,2:T(2,128)(2,1)} copy(bf16[1,1296,128]{2,1,0:T(8,128)(2,1)} %collective-permute-done.6) | data formatting | bytes 663552 | tf_op jit(solution)/shard_map/ppermute | solution.py:17
  173.8 3.4 %maximum_convert_fusion = f32[6,1296,128]{1,0,2:T(8,128)S(1)} fusion(bf16[1,1296,128]{1,0,2:T(2,128)(2,1)S(1)} %copy.80, bf16[4,1296,128]{1,0,2:T(4,128)(2,1)S(1)} %fusion.22, bf16[1,1296,128]{1,0,2:T(2,128)(2,1)} %copy.79), kind=kLoop, calls=%fused_computation.24 | loop fusion | flops 5971968 | bytes 5971968 | tf_op jit(solution)/shard_map/convert_element_type | solution.py:101
  177.2 5.0 %fusion.47 = (f32[5,1296,128]{1,0,2:T(8,128)}, f32[5,1296,128]{1,0,2:T(8,128)}) fusion(f32[6,1296,128]{1,0,2:T(8,128)S(1)} %maximum_convert_fusion), kind=kLoop, calls=%fused_computation.101 | loop fusion | bytes 13271040 | tf_op jit(solution)/shard_map/slice | solution.py:118
  182.1 6.3 %copy.81 = f32[5,1296,128]{2,0,1:T(8,128)} copy(f32[5,1296,128]{1,0,2:T(8,128)} %get-tuple-element.8) | data formatting | bytes 6635520 | tf_op jit(solution)/shard_map/slice | solution.py:118
  188.4 6.4 %copy.82 = f32[5,1296,128]{2,0,1:T(8,128)} copy(f32[5,1296,128]{1,0,2:T(8,128)} %get-tuple-element.7) | data formatting | bytes 6635520 | tf_op jit(solution)/shard_map/slice | solution.py:118
  194.8 5.5 %fusion.6 = f32[5,36,36,128]{3,0,2,1:T(8,128)S(1)} fusion(f32[5,36,36,128]{3,0,2,1:T(8,128)} %bitcast.51, f32[5,36,36,128]{3,0,2,1:T(8,128)} %bitcast.52, f32[5,128]{1,0:T(8,128)S(1)} %get-tuple-element.17, f32[36,36]{1,0:T(8,128)S(1)} %get-tuple-element.30, f32[5,128]{1,0:T(8,128)S(1)} %get-tuple-element.16), kind=kLoop, calls=%fused_computation.12 | loop fusion | flops 5806080 | bytes 9963584 | tf_op jit(solution)/shard_map/mul | solution.py:117
  200.3 2.1 fusion.15
  202.4 0.2 slice.240
  202.6 0.7 copy-done
  203.3 0.0 copy-done.1
  203.3 1.0 fusion.17
  204.3 0.2 slice.243
  204.5 2.1 %fusion.23 = bf16[36,36,4,128]{3,2,1,0:T(4,128)(2,1)} fusion(f32[4,128]{1,0:T(4,128)S(1)} %get-tuple-element.27, f32[4,36,36,128]{3,0,2,1:T(4,128)S(1)} %fusion.15, f32[4,36,36,128]{3,0,2,1:T(4,128)S(1)} %fusion.17, f32[4,36,35,128]{3,0,2,1:T(4,128)S(1)} %slice.243, f32[4,36,1,128]{3,0,2,1:T(4,128)S(1)} %slice.242), kind=kLoop, calls=%fused_computation.39 | loop fusion | flops 3317760 | bytes 9291776 | tf_op jit(solution)/shard_map/transpose | solution.py:140
  (47 shorter events, 0.4 us)
Async XLA Ops:
  6.8 9.3 %copy-start.3 = (bf16[2,1,8,128]{3,2,1,0:T(8,128)(2,1)S(1)}, bf16[2,1,8,128]{3,2,1,0:T(8,128)(2,1)}, u32[]{:S(2)}) copy-start(bf16[2,1,8,128]{3,2,1,0:T(8,128)(2,1)} %param.11) | copy-start | bytes 12292
  6.8 60.4 %copy-start.5 = (s32[4,1]{0,1:T(1,128)S(1)}, s32[4,1]{0,1:T(1,128)}, u32[]{:S(2)}) copy-start(s32[4,1]{0,1:T(1,128)} %param.13) | copy-start | bytes 52
  6.8 60.4 %copy-start.6 = (s32[4,1]{0,1:T(1,128)S(1)}, s32[4,1]{0,1:T(1,128)}, u32[]{:S(2)}) copy-start(s32[4,1]{0,1:T(1,128)} %param.12) | copy-start | bytes 52
  6.8 61.1 %copy-start.4 = (s32[4,128]{1,0:T(4,128)S(1)}, s32[4,128]{1,0:T(4,128)}, u32[]{:S(2)}) copy-start(s32[4,128]{1,0:T(4,128)} %param.15) | copy-start | bytes 6148
  6.8 72.4 %copy-start.2 = (s32[4,128]{1,0:T(4,128)S(1)}, s32[4,128]{1,0:T(4,128)}, u32[]{:S(2)}) copy-start(s32[4,128]{1,0:T(4,128)} %param.14) | copy-start | bytes 6148
  8.4 70.8 %all-to-all-start = ((bf16[8,64,1,1296]{3,1,2,0:T(8,128)(2,1)}), bf16[8,64,1,1296]{3,1,2,0:T(8,128)(2,1)S(1)}, u32[]{:S(2)}, u32[]{:S(2)}) async-start(bf16[8,64,1,1296]{3,1,2,0:T(8,128)(2,1)} %bitcast.2), calls=%async_computation | async-start | bytes 2883584 | tf_op jit(solution)/shard_map/all_to_all | solution.py:82
  67.9 22.0 %collective-permute-start.5 = (bf16[1,3,128]{2,0,1:T(2,128)(2,1)S(1)}, bf16[1,3,128]{2,0,1:T(2,128)(2,1)S(1)}, u32[]{:S(2)}, u32[]{:S(2)}) collective-permute-start(bf16[1,3,128]{2,0,1:T(2,128)(2,1)S(1)} %get-tuple-element.23), channel_id=1, source_target_pairs={{1,0},{2,1},{3,2},{4,3},{5,4},{6,5},{7,6},{9,8},{10,9},{11,10},{12... | collective-permute-start | bytes 2312 | tf_op jit(solution)/shard_map/ppermute | solution.py:18
  69.2 20.7 %collective-permute-start.4 = (bf16[1,3,128]{2,0,1:T(2,128)(2,1)S(1)}, bf16[1,3,128]{2,0,1:T(2,128)(2,1)S(1)}, u32[]{:S(2)}, u32[]{:S(2)}) collective-permute-start(bf16[1,3,128]{2,0,1:T(2,128)(2,1)S(1)} %get-tuple-element.22), channel_id=1, source_target_pairs={{0,1},{1,2},{2,3},{3,4},{4,5},{5,6},{6,7},{8,9},{9,10},{10,11},{11... | collective-permute-start | bytes 2312 | tf_op jit(solution)/shard_map/ppermute | solution.py:17
  73.6 16.0 %collective-permute-start.1 = (bf16[4,3,1]{2,0,1:T(4,128)(2,1)S(1)}, bf16[4,3,1]{2,0,1:T(4,128)(2,1)S(1)}, u32[]{:S(2)}, u32[]{:S(2)}) collective-permute-start(bf16[4,3,1]{2,0,1:T(4,128)(2,1)S(1)} %get-tuple-element.21), channel_id=1, source_target_pairs={{8,0},{16,8},{24,16},{32,24},{40,32},{48,40},{56,48},{64,56},{72,6... | collective-permute-start | bytes 80 | tf_op jit(solution)/shard_map/ppermute | solution.py:18
  75.9 13.6 %collective-permute-start = (bf16[4,3,1]{2,0,1:T(4,128)(2,1)S(1)}, bf16[4,3,1]{2,0,1:T(4,128)(2,1)S(1)}, u32[]{:S(2)}, u32[]{:S(2)}) collective-permute-start(bf16[4,3,1]{2,0,1:T(4,128)(2,1)S(1)} %get-tuple-element.20), channel_id=1, source_target_pairs={{0,8},{8,16},{16,24},{24,32},{32,40},{40,48},{48,56},{56,64},{64,7... | collective-permute-start | bytes 80 | tf_op jit(solution)/shard_map/ppermute | solution.py:17
  81.2 44.3 %all-to-all-start.1 = ((bf16[8,64,1,1296]{3,0,2,1:T(8,128)(2,1)}), bf16[8,64,1,1296]{3,0,2,1:T(8,128)(2,1)S(1)}, u32[]{:S(2)}, u32[]{:S(2)}) async-start(bf16[8,64,1,1296]{3,0,2,1:T(8,128)(2,1)} %copy.69), calls=%async_computation.1 | async-start | bytes 2883584 | tf_op jit(solution)/shard_map/all_to_all | solution.py:83
  130.6 20.8 %collective-permute-start.3 = (bf16[4,1296,1]{1,0,2:T(4,128)(2,1)}, bf16[4,1296,1]{1,0,2:T(4,128)(2,1)}, u32[]{:S(2)}, u32[]{:S(2)}) collective-permute-start(bf16[4,1296,1]{1,0,2:T(4,128)(2,1)} %get-tuple-element.10), channel_id=1, source_target_pairs={{8,0},{16,8},{24,16},{32,24},{40,32},{48,40},{56,48},{64,56},{72,6... | collective-permute-start | bytes 31112 | tf_op jit(solution)/shard_map/ppermute | solution.py:18
  133.9 20.9 %collective-permute-start.2 = (bf16[4,1296,1]{1,0,2:T(4,128)(2,1)}, bf16[4,1296,1]{1,0,2:T(4,128)(2,1)}, u32[]{:S(2)}, u32[]{:S(2)}) collective-permute-start(bf16[4,1296,1]{1,0,2:T(4,128)(2,1)} %get-tuple-element.9), channel_id=1, source_target_pairs={{0,8},{8,16},{16,24},{24,32},{32,40},{40,48},{48,56},{56,64},{64,7... | collective-permute-start | bytes 31112 | tf_op jit(solution)/shard_map/ppermute | solution.py:17
  143.6 24.9 %collective-permute-start.7 = (bf16[1,1296,128]{2,1,0:T(8,128)(2,1)}, bf16[1,1296,128]{2,1,0:T(8,128)(2,1)}, u32[]{:S(2)}, u32[]{:S(2)}) collective-permute-start(bf16[1,1296,128]{2,1,0:T(8,128)(2,1)} %copy.78), channel_id=1, source_target_pairs={{1,0},{2,1},{3,2},{4,3},{5,4},{6,5},{7,6},{9,8},{10,9},{11,10},{12... | collective-permute-start | bytes 995336 | tf_op jit(solution)/shard_map/ppermute | solution.py:18
  146.6 24.2 %collective-permute-start.6 = (bf16[1,1296,128]{2,1,0:T(8,128)(2,1)}, bf16[1,1296,128]{2,1,0:T(8,128)(2,1)}, u32[]{:S(2)}, u32[]{:S(2)}) collective-permute-start(bf16[1,1296,128]{2,1,0:T(8,128)(2,1)} %copy.77), channel_id=1, source_target_pairs={{0,1},{1,2},{2,3},{3,4},{4,5},{5,6},{6,7},{8,9},{9,10},{10,11},{11... | collective-permute-start | bytes 995336 | tf_op jit(solution)/shard_map/ppermute | solution.py:17
  188.4 11.9 %slice-start = ((s8[5308416]{0:T(1024)(128)(4,1)}), s8[1114112]{0:T(1024)(128)(4,1)S(1)}, s32[]{:S(2)}) async-start(s8[5308416]{0:T(1024)(128)(4,1)} %bitcast.49), calls=%async_computation.2 | async-start | bytes 2228224
  194.8 5.5 %slice-start.1 = ((s8[5308416]{0:T(1024)(128)(4,1)}), s8[4194304]{0:T(1024)(128)(4,1)S(1)}, s32[]{:S(2)}) async-start(s8[5308416]{0:T(1024)(128)(4,1)} %bitcast.49), calls=%async_computation.3 | async-start | bytes 8388608
  202.4 0.9 copy-start
  202.4 0.9 copy-start.1
where the time goes:
time: 209 us; the launch traced here: 207 us
  blocking collectives  51.1 us (24%)
  local copies, waits for them, and re-layouts  47.4 us (23%)
  starting transfers between devices  39 us (19%)
  waiting for transfers between devices  34.7 us (17%)
  other arithmetic  34 us (16%)
    all_gather x1, blocking collectives, body(): piece = lax.all_gather(ocean_current, 'lon', axis=2, tiled=True)  51.1 us
    all_to_all x1, waiting for transfers between devices, body(): lax.all_to_all(section, 'lon', split_axis=1, concat_axis=1, tiled=True)  34.7 us
    ppermute x4, starting transfers between devices, with_halo(): before = lax.ppermute(last, axis, up)  15.2 us
    slice x2, local copies, waits for them, and re-layouts, body(): tall[1:]  11.4 us
    ppermute x4, starting transfers between devices, with_halo(): after = lax.ppermute(leading, axis, down)  8.23 us
    all_to_all x1, starting transfers between devices, body(): lax.all_to_all(section, 'lon', split_axis=1, concat_axis=1, tiled=True)  7.94 us
    all_to_all x1, starting transfers between devices, body(): lax.all_to_all(packed, 'lat', split_axis=0, concat_axis=0, tiled=True)  7.65 us
    concatenate x4, local copies, waits for them, and re-layouts, with_halo(): shard = jnp.concatenate([before, shard, after], axis=dim)  6.81 us
  transfers between devices with their start and end apart: 10, of which 1 were waited for; matrix products, arithmetic and copies ran while one was open for 16% of the time, Pallas kernels for 0%

commit v1 on v0

v1 whole, which is shorter than its diff:
```python
import functools
import math

import jax
import jax.numpy as jnp
import numpy as np
from jax import lax
from jax.experimental import pallas as pl
from jax.experimental.pallas import tpu as pltpu
from jax.sharding import PartitionSpec as P

NF, ND = 36, 36
SPEC = NF * ND
PAD = 1408
CELLS = 512
NK, NZX = 16, 32
CHUNKS = ((0, 384), (384, 384), (768, 384), (1152, 256))
SOURCE_GROUPS = ((0, 3), (3, 6), (6, 8), (8, 9))
READY_GROUPS = ((0, 2), (2, 5), (5, 8), (8, 9))
NC = len(CHUNKS)
GROUP = 4 * ND
HALF = ND // 2
MESH = pl.DeviceIdType.MESH
TURN_SCALE = 2.5
F32, BF16 = jnp.float32, jnp.bfloat16


def iota(shape, axis):
    return lax.broadcasted_iota(jnp.int32, shape, axis)


def onehot(cond):
    return jnp.where(cond, 1.0, 0.0).astype(BF16)


def dot(a, b, ca, cb):
    return lax.dot_general(a, b, (((ca,), (cb,)), ((), ())), preferred_element_type=F32)


def drain(ref, sem):
    pltpu.make_async_copy(ref, ref, sem).wait()


def kernel(
    spec_ref, wind_ref, dirs_ref, fscale_ref, cg_ref, cur_ref, owner_ref, slot_ref, source_ref, mask_ref,
    out_ref,
    s_ref, e_ref, hp_ref, o_ref, x1, y1, y2, z, ns_out, ns_in, ew_out, ew_in, cur_all, aux_out, aux_in,
    face_x, face_y, turn_ref, sea_ref, pick_ref,
    p1_send, p1_recv, p2_send, p2_recv, h_send, h_recv, c_sem, a_send, a_recv,
):
    lon, lat = lax.axis_index("lon"), lax.axis_index("lat")
    n_lon, n_lat = NZX * 2, NK // 2
    zx, core = lon // 2, lon % 2
    me = lat * 2 + core
    north, south = (lat + 1) % n_lat, (lat + n_lat - 1) % n_lat
    east, west = (lon + 1) % n_lon, (lon + n_lon - 1) % n_lon
    sides = ((lon, north), (lon, south), (east, lat), (west, lat))

    def dev(lo, la):
        return {"lon": lo, "lat": la}

    barrier = pltpu.get_barrier_semaphore()

    def greet1(i, _):
        k = (me + i) % NK
        pl.semaphore_signal(barrier, inc=1, device_id=dev(zx * 2 + k % 2, k // 2), device_id_type=MESH)
        return 0

    def greet2(i, _):
        t = (zx + i) % NZX
        pl.semaphore_signal(barrier, inc=1, device_id=dev(t * 2 + core, lat), device_id_type=MESH)
        return 0

    lax.fori_loop(1, NK, greet1, 0)
    lax.fori_loop(1, NZX, greet2, 0)
    for lo, la in ((east, lat), (west, lat)):
        pl.semaphore_signal(barrier, inc=1, device_id=dev(lo, la), device_id_type=MESH)

    def add(f, acc):
        return acc + spec_ref[f].astype(F32)

    total = lax.fori_loop(0, NF, add, jnp.zeros((ND, CELLS), F32))
    m0 = jnp.sum(total, axis=0, keepdims=True) / SPEC
    loss0 = 0.3 * (m0 / 0.5) ** 2
    cosd = jnp.concatenate([dirs_ref[:, :128]] * 4, axis=1)
    sind = jnp.concatenate([dirs_ref[:, 128:]] * 4, axis=1)
    proj = wind_ref[0:1, :] * cosd + wind_ref[1:2, :] * sind
    s_ref[SPEC:PAD, :] = jnp.zeros((PAD - SPEC, CELLS), F32)

    row, col = iota((CELLS, CELLS), 0), iota((CELLS, CELLS), 1)
    k, t = row // NZX, row % NZX
    by_dest = onehot(col == (k // 2) * n_lon + t * 2 + k % 2)
    regroup = onehot((row // NK == col % NZX) & (row % NK == col // NZX))

    def source(g, _):
        rows = s_ref.at[pl.ds(pl.multiple_of(g * GROUP, 16), GROUP), :]
        for i in range(4):
            f = g * 4 + i
            drive = jnp.maximum(proj * fscale_ref[f] - 1.0, 0.0)
            gain = 0.5 * jnp.tanh(0.2 * drive)
            rows[ND * i : ND * (i + 1), :] = spec_ref[f].astype(F32) * jnp.exp(gain - fscale_ref[NF + f] * loss0)
        return 0

    def send1(c):
        def one(i, _):
            k = (me + i) % NK
            pltpu.make_async_remote_copy(
                src_ref=x1[c].at[k], dst_ref=y1[c].at[me], send_sem=p1_send.at[c], recv_sem=p1_recv.at[c],
                device_id=dev(zx * 2 + k % 2, k // 2), device_id_type=MESH,
            ).start()
            return 0

        lax.fori_loop(1, NK, one, 0)
        pltpu.make_async_copy(x1[c].at[me], y1[c].at[me], p1_recv.at[c]).start()

    def send2(c):
        def one(i, _):
            t = (zx + i) % NZX
            pltpu.make_async_remote_copy(
                src_ref=y2[c].at[t], dst_ref=z[c].at[zx], send_sem=p2_send.at[c], recv_sem=p2_recv.at[c],
                device_id=dev(t * 2 + core, lat), device_id_type=MESH,
            ).start()
            return 0

        lax.fori_loop(1, NZX, one, 0)
        pltpu.make_async_copy(y2[c].at[zx], z[c].at[zx], p2_recv.at[c]).start()

    for c, (at, width) in enumerate(CHUNKS):
        lax.fori_loop(*SOURCE_GROUPS[c], source, 0)
        values = s_ref[at : at + width, :].astype(BF16)
        x1[c][...] = dot(by_dest, values, 1, 1).astype(BF16).reshape(NK, NZX, width)
        if c == 0:
            pl.semaphore_wait(barrier, NK - 1 + NZX - 1 + 2)
        send1(c)
        if c == 0:
            swap = pltpu.make_async_remote_copy(
                src_ref=cur_ref, dst_ref=cur_all.at[zx, core], send_sem=c_sem.at[0], recv_sem=c_sem.at[1],
                device_id=dev(zx * 2 + 1 - core, lat), device_id_type=MESH,
            )
            swap.start()
            pltpu.make_async_copy(cur_ref, cur_all.at[zx, core], c_sem.at[1]).start()

    drain(cur_all.at[zx], c_sem.at[1])

    def share(i, _):
        t = (zx + i) % NZX
        pltpu.make_async_remote_copy(
            src_ref=cur_all.at[zx], dst_ref=cur_all.at[zx], send_sem=c_sem.at[2], recv_sem=c_sem.at[3],
            device_id=dev(t * 2 + core, lat), device_id_type=MESH,
        ).start()
        return 0

    lax.fori_loop(1, NZX, share, 0)

    q = source_ref[...]
    where = ((q % n_lon) // 2) * NK + (q // n_lon) * 2 + q % 2
    where = jnp.where(mask_ref[...] > 0, where, -1)
    slots = iota((CELLS, 128), 0)
    for y in range(4):
        pick_ref[:, 128 * y : 128 * (y + 1)] = onehot(slots == where[y : y + 1, :])
    both = jnp.concatenate([where, where, jnp.full((8, 128), -1, jnp.int32)], axis=0)
    edge_row = iota((16, 1), 0)
    edge = jnp.where(edge_row < 4, both[:, 127:128], both[:, 0:1])
    edge_pick = onehot(iota((16, CELLS), 1) == edge)
    pr, pc = iota((32, CELLS), 0), iota((32, CELLS), 1)
    place = onehot(((pr < 4) & (pc == pr * 128)) | ((pr >= 20) & (pr < 24) & (pc == (pr - 20) * 128 + 127)))

    def halo_copies(c):
        ew = (ew_out[c], ew_in[c])
        ns = (ns_out[c], ns_in[c])
        parts = (
            (ns[0].at[1], ns[1].at[1]),
            (ns[0].at[0], ns[1].at[0]),
            (ew[0], ew[1].at[0]),
            (ew[0], ew[1].at[1]),
        )
        return [
            pltpu.make_async_remote_copy(
                src_ref=src, dst_ref=dst, send_sem=h_send.at[c, d], recv_sem=h_recv.at[c, d],
                device_id=dev(*sides[d]), device_id_type=MESH,
            )
            for d, (src, dst) in enumerate(parts)
        ]

    def aux_copies():
        return [
            pltpu.make_async_remote_copy(
                src_ref=aux_out, dst_ref=aux_in.at[d], send_sem=a_send.at[d], recv_sem=a_recv.at[d],
                device_id=dev(*sides[d]), device_id_type=MESH,
            )
            for d in range(4)
        ]

    def pick(c):
        at, width = CHUNKS[c]
        drain(z[c], p2_recv.at[c])
        got = z[c][...].reshape(CELLS, width)
        ew_out[c][...] = dot(edge_pick, got, 1, 0).astype(BF16)
        energy = dot(got, pick_ref[...], 0, 0)
        for y in range(4):
            e_ref[1 + y, at : at + width, :] = energy[:, 128 * y : 128 * (y + 1)]
        ns_out[c][0] = energy[:, :128].astype(BF16)
        ns_out[c][1] = energy[:, 384:].astype(BF16)
        for copy in halo_copies(c):
            copy.start()

    def send_aux():
        drain(cur_all.at[pl.ds(0, NZX - 1)], c_sem.at[3])
        wanted = owner_ref[...] * 16 + slot_ref[...]
        wanted = jnp.concatenate([wanted, wanted + 8, jnp.full((8, 1), -1, jnp.int32)], axis=0)
        blocks = onehot(iota((16, NZX * 32), 1) == wanted)
        found = dot(blocks, cur_all[...].reshape(NZX * 32, 128), 1, 0)
        sea = jnp.concatenate([jnp.zeros((8, 128), F32), mask_ref[...].astype(F32), jnp.zeros((4, 128), F32)], axis=0)
        aux_out[...] = (found + sea).astype(BF16)
        for copy in aux_copies():
            copy.start()

    def prepare():
        for copy in aux_copies():
            copy.wait_recv()
        own = aux_out[...].astype(F32)
        to_south, to_north, to_west, to_east = [aux_in[d].astype(F32) for d in range(4)]
        to_north = to_north * jnp.where(lat < n_lat - 1, 1.0, 0.0)
        to_south = to_south * jnp.where(lat > 0, 1.0, 0.0)
        lane = iota((16, 128), 1)
        right = jnp.where(lane == 127, pltpu.roll(to_east, 127, 1), pltpu.roll(own, 127, 1))
        left = jnp.where(lane == 0, pltpu.roll(to_west, 1, 1), pltpu.roll(own, 1, 1))
        u, v, m = own[0:4], own[4:8], own[8:12]
        ur, vr, mr = right[0:4], right[4:8], right[8:12]
        ul, vl, ml = left[0:4], left[4:8], left[8:12]
        ut = jnp.concatenate([to_south[3:4], u, to_north[0:1]], axis=0)
        vt = jnp.concatenate([to_south[7:8], v, to_north[4:5]], axis=0)
        mt = jnp.concatenate([to_south[11:12], m, to_north[8:9]], axis=0)
        fur, ful = 0.5 * (u + ur), 0.5 * (ul + u)
        oxr, oxl = m * mr, ml * m
        fv, oy = 0.5 * (vt[0:5] + vt[1:6]), mt[0:5] * mt[1:6]
        ux, vx = 0.5 * (ur - ul), 0.5 * (vr - vl)
        uy, vy = 0.5 * (ut[2:6] - ut[0:4]), 0.5 * (vt[2:6] - vt[0:4])
        wide = lambda a: jnp.broadcast_to(a, (8, 128))
        for y in range(4):
            for n, a in enumerate((fur, oxr, ful, oxl)):
                face_x[y, n] = wide(a[y : y + 1])
            sea_ref[y] = wide(m[y : y + 1])
        for y in range(5):
            face_y[y, 0] = wide(fv[y : y + 1])
            face_y[y, 1] = wide(oy[y : y + 1])
        for d in range(HALF):
            phi = (d + 1) * 2.0 * math.pi / ND
            fs, fc = math.sin(phi), math.cos(phi)
            turn = TURN_SCALE * ((fs * fc) * (ux - vy) + (fs * fs) * uy - (fc * fc) * vx)
            for y in range(4):
                turn_ref[y, d] = wide(turn[y : y + 1])

    def arrive(c):
        at, width = CHUNKS[c]
        for copy in halo_copies(c):
            copy.wait_recv()
        e_ref[0, at : at + width, :] = ns_in[c][1].astype(F32)
        e_ref[5, at : at + width, :] = ns_in[c][0].astype(F32)
        placed = dot(ew_in[c][...].reshape(32, width), place, 0, 0)
        for y in range(4):
            hp_ref[y, at : at + width, :] = placed[:, 128 * y : 128 * (y + 1)]

    lane = iota((8, 128), 1)

    def advance(step, _):
        g, y = step // 4, step % 4
        base = g * GROUP
        cg = cg_ref[g]
        fur, oxr, ful, oxl = [face_x[y, n] for n in range(4)]
        fvs, oys, fvn, oyn = face_y[y, 0], face_y[y, 1], face_y[y + 1, 0], face_y[y + 1, 1]
        sea = sea_ref[y]

        def flux(speed, here, there, is_open):
            return is_open * (speed * jnp.where(speed > 0.0, here, there))

        moved = []
        for d in range(HALF):
            theta = (d + 0.5) * 2.0 * math.pi / ND
            rows = pl.ds(base + d, 8, stride=HALF)
            here, up, down = e_ref[y + 1, rows, :], e_ref[y + 2, rows, :], e_ref[y, rows, :]
            halo = hp_ref[y, rows, :]
            right = jnp.where(lane == 127, halo, pltpu.roll(here, 127, 1))
            left = jnp.where(lane == 0, halo, pltpu.roll(here, 1, 1))
            sx, sy = cg * math.cos(theta), cg * math.sin(theta)
            div_x = flux(sx + fur, here, right, oxr) - flux(sx + ful, left, here, oxl)
            div_y = flux(sy + fvn, here, up, oyn) - flux(sy + fvs, down, here, oys)
            moved.append(here - div_x - div_y)
        half = iota((8, 128), 0) % 2
        swap = lambda a: jnp.where(half == 0, pltpu.roll(a, 7, 0), pltpu.roll(a, 1, 0))
        first = swap(moved[0])
        bent = []
        for d in range(HALF):
            turn = turn_ref[y, d]
            bent.append(turn * jnp.where(turn > 0.0, moved[d], moved[d + 1] if d + 1 < HALF else first))
        before = swap(bent[-1])
        for d in range(HALF):
            value = (moved[d] - (bent[d] - before)) * sea
            o_ref[pl.ds(g * (4 * GROUP) + d * 4 + y, 8, stride=4 * HALF), :] = value
            before = bent[d]
        return 0

    def finish(g, _):
        rows = pl.ds(pl.multiple_of(g * 4 * GROUP, 16), 4 * GROUP)
        out_ref[rows, :] = o_ref[rows, :].astype(BF16)
        return 0

    def propagate(c):
        first, last = READY_GROUPS[c]
        arrive(c)
        lax.fori_loop(first * 4, last * 4, advance, 0)
        lax.fori_loop(first, last, finish, 0)

    for c, (at, width) in enumerate(CHUNKS):
        drain(y1[c], p1_recv.at[c])
        y2[c][...] = dot(regroup, y1[c][...].reshape(CELLS, width), 1, 0).astype(BF16).reshape(NZX, NK, width)
        send2(c)
        if c == 0:
            send_aux()
        if c == 1:
            prepare()
        if c >= 1:
            pick(c - 1)
        if c >= 2:
            propagate(c - 2)
    pick(NC - 1)
    propagate(NC - 2)
    propagate(NC - 1)

    for c in range(NC):
        drain(x1[c].at[pl.ds(0, NK - 1)], p1_send.at[c])
        drain(y2[c].at[pl.ds(0, NZX - 1)], p2_send.at[c])
        for copy in halo_copies(c):
            copy.wait_send()
    drain(cur_ref, c_sem.at[0])
    drain(cur_all.at[pl.ds(0, NZX - 1)], c_sem.at[2])
    for copy in aux_copies():
        copy.wait_send()


def tables():
    ratio = 1.1 ** np.arange(NF)
    theta = (np.arange(ND) + 0.5) * 2.0 * np.pi / ND
    dirs = np.repeat(np.stack([np.cos(theta), np.sin(theta)], axis=1), 128, axis=1)
    fscale = np.concatenate([ratio / 44.6, ratio / ratio[-1]])
    speed = (0.53 / ratio).reshape(9, 4, 1) * np.array([1.0, -1.0]).reshape(1, 1, 2)
    cg = np.repeat(speed.reshape(9, 8, 1), 128, axis=2)
    return [np.asarray(a, np.float32) for a in (dirs, fscale, cg)]


def body(spec_pts, wind_u, wind_v, ocean_current, block_owner, block_slot, cell_source, land_mask):
    vmem, smem = pl.BlockSpec(memory_space=pltpu.VMEM), pl.BlockSpec(memory_space=pltpu.SMEM)
    dirs, fscale, cg = tables()
    wind = jnp.stack([wind_u, wind_v])
    per_chunk = lambda shape: [pltpu.VMEM(shape(w), BF16) for _, w in CHUNKS]
    dma = pltpu.SemaphoreType.DMA
    out = pl.pallas_call(
        kernel,
        out_shape=jax.ShapeDtypeStruct((SPEC * 4, 128), BF16),
        in_specs=[vmem, vmem, vmem, smem, vmem, vmem, vmem, vmem, vmem, vmem],
        out_specs=vmem,
        scratch_shapes=[
            pltpu.VMEM((PAD, CELLS), F32),
            pltpu.VMEM((6, PAD, 128), F32),
            pltpu.VMEM((4, PAD, 128), F32),
            pltpu.VMEM((SPEC * 4, 128), F32),
            per_chunk(lambda w: (NK, NZX, w)),
            per_chunk(lambda w: (NK, NZX, w)),
            per_chunk(lambda w: (NZX, NK, w)),
            per_chunk(lambda w: (NZX, NK, w)),
            per_chunk(lambda w: (2, w, 128)),
            per_chunk(lambda w: (2, w, 128)),
            per_chunk(lambda w: (16, w)),
            per_chunk(lambda w: (2, 16, w)),
            pltpu.VMEM((NZX, 2, 16, 128), BF16),
            pltpu.VMEM((16, 128), BF16),
            pltpu.VMEM((4, 16, 128), BF16),
            pltpu.VMEM((4, 4, 8, 128), F32),
            pltpu.VMEM((5, 2, 8, 128), F32),
            pltpu.VMEM((4, HALF, 8, 128), F32),
            pltpu.VMEM((4, 8, 128), F32),
            pltpu.VMEM((CELLS, CELLS), BF16),
            dma((NC,)), dma((NC,)), dma((NC,)), dma((NC,)), dma((NC, 4)), dma((NC, 4)), dma((4,)), dma((4,)), dma((4,)),
        ],
        compiler_params=pltpu.CompilerParams(
            collective_id=0, has_side_effects=True, vmem_limit_bytes=48 * 2**20
        ),
    )(
        spec_pts, wind, jnp.asarray(dirs), jnp.asarray(fscale), jnp.asarray(cg),
        ocean_current.reshape(16, 128), block_owner, block_slot, cell_source, land_mask,
    )
    return out.reshape(NF, ND, 4, 128)


def solution(mesh):
    return jax.shard_map(
        body,
        mesh=mesh,
        in_specs=(
            P(None, None, ("lon", "lat")),
            P(("lon", "lat")),
            P(("lon", "lat")),
            P(None, "lat", "lon", None),
            P("lat", "lon"),
            P("lat", "lon"),
            P("lat", "lon"),
            P("lat", "lon"),
        ),
        out_specs=P(None, None, "lat", "lon"),
        check_vma=False,
    )
```

time: 209 us -> 82.2 us (0.39)
  Pallas kernels: 0 us -> 72.1 us
  blocking collectives: 51.1 us -> 0 us
  local copies, waits for them, and re-layouts: 47.4 us -> 8.16 us
  starting transfers between devices: 39 us -> 0 us
  waiting for transfers between devices: 34.7 us -> 0 us
  other arithmetic: 34 us -> 0.71 us
    pallas_call x0 -> x1, Pallas kernels: none -> 72.1 us  [body(): pl.pallas_call(kernel, out_shape=jax.ShapeDtypeStruct((SPEC * 4, 128), BF...]
    all_gather x1 -> x0, blocking collectives: 51.1 us -> none  [body(): piece = lax.all_gather(ocean_current, 'lon', axis=2, tiled=True)]
    all_to_all x2 -> x0, waiting for transfers between devices: 34.7 us -> none  [the longest x1 34.7 us: body(): lax.all_to_all(section, 'lon', split_axis=1, concat_axis=1, tiled=True)]
    slice x15 -> x0, local copies, waits for them, and re-layouts: 25.7 us -> none  [the longest x2 11.4 us: body(): tall[1:]]
    ppermute x8 -> x0, starting transfers between devices: 23.4 us -> none  [the longest x4 15.2 us: with_halo(): before = lax.ppermute(last, axis, up)]
    all_to_all x2 -> x0, starting transfers between devices: 15.6 us -> none  [the longest x1 7.94 us: body(): lax.all_to_all(section, 'lon', split_axis=1, concat_axis=1, tiled=True)]
    mul x13 -> x0, other arithmetic: 14.3 us -> none  [the longest x1 5.55 us: body(): open_x[:, None, None, :]]
    convert_element_type x6 -> x0, other arithmetic: 10.9 us -> none  [the longest x1 4.83 us: body(): wide_tile.astype(jnp.float32).reshape(lat_rows, freqs, dirs, lon_cells + 2)]
  transfers between devices with their start and end apart: 10 -> 0, of which waited for: 1 -> 0; matrix products, arithmetic and copies ran while one was open for 16% -> 0% of each run, Pallas kernels for 0% -> 0%
where the time goes in v1:
time: 82.2 us; the launch traced here: 81 us
  Pallas kernels  72.1 us (88%)
  local copies, waits for them, and re-layouts  8.16 us (10%)
    pallas_call x1, Pallas kernels, body(): pl.pallas_call(kernel, out_shape=jax.ShapeDtypeStruct((SPEC * 4, 128), BF...  72.1 us
    unnamed x17, local copies, waits for them, and re-layouts  8.16 us

profile of v1, /device:TPU:1, one launch (start us, length us, event | category | flops | bytes accessed | tf_op | source)
XLA Modules:
  0.0 81.0 jit_solution(676638619951879415)
XLA Ops:
  0.0 0.7 copy.12.owner_ref
  0.7 0.7 copy.13.slot_ref
  1.5 0.7 pad_maximum_fusion.wind_ref
  2.2 0.0 copy-start
  2.2 1.4 %copy-done = bf16[36,36,512]{2,1,0:T(8,128)(2,1)S(1)} copy-done((bf16[36,36,512]{2,1,0:T(8,128)(2,1)S(1)}, bf16[36,36,512]{2,1,0:T(8,128)(2,1)}, u32[]{:S(2)}) %copy-start) | copy-done | bytes 1327128
  3.6 0.0 copy-start.1
  3.6 0.8 copy-done.1
  4.3 0.0 copy-start.2
  4.3 0.8 copy-done.2
  5.1 0.0 copy-start.3
  5.1 0.7 copy-done.3
  5.8 0.0 copy-start.4
  5.8 0.7 copy-done.4
  6.5 0.0 copy-start.5
  6.5 0.7 copy-done.5
  7.2 0.0 copy-start.6
  7.2 0.7 copy-done.6
  7.8 72.1 %shard_map.109 = bf16[5184,128]{1,0:T(8,128)(2,1)S(1)} custom-call(bf16[36,36,512]{2,1,0:T(8,128)(2,1)S(1)} %copy-done, f32[2,512]{1,0:T(2,128)S(1)} %pad_maximum_fusion.wind_ref, f32[36,256]{1,0:T(8,128)S(1)} %copy-done.1, f32[72]{0:T(128)S(1)} %copy-done.6, f32[9,8,128]{2,1,0:T(8,128)S(1)} %copy-done.2, bf16[16,128]{1,0:T(8,128)(2,1)S(1)} %bitcast.5, ...), custom_call_target="tpu_custom_call" | custom-call | tf_op jit(solution)/shard_map/pallas_call | solution.py:357
  79.9 1.1 %copy.15 = bf16[36,36,4,128]{3,2,1,0:T(4,128)(2,1)} copy(bf16[36,36,4,128]{3,2,1,0:T(4,128)(2,1)S(1)} %bitcast.4) | data formatting | bytes 2654208
Async XLA Ops:
  2.2 1.4 %copy-start = (bf16[36,36,512]{2,1,0:T(8,128)(2,1)S(1)}, bf16[36,36,512]{2,1,0:T(8,128)(2,1)}, u32[]{:S(2)}) copy-start(bf16[36,36,512]{2,1,0:T(8,128)(2,1)} %spec_ref.1) | copy-start | bytes 3981316
  3.6 0.8 copy-start.1
  4.3 0.8 copy-start.2
  5.1 0.7 copy-start.3
  5.8 0.7 copy-start.4
  6.5 0.7 copy-start.5
  7.2 0.7 copy-start.6

commit v2 on v1

--- a/solution.py
+++ b/solution.py
@@ -14,11 +14,21 @@
 PAD = 1408
 CELLS = 512
 NK, NZX = 16, 32
-CHUNKS = ((0, 384), (384, 384), (768, 384), (1152, 256))
-SOURCE_GROUPS = ((0, 3), (3, 6), (6, 8), (8, 9))
-READY_GROUPS = ((0, 2), (2, 5), (5, 8), (8, 9))
+WIDTHS = (512, 128, 640, 128)
+FIRST = (0, 0, 1, 1)
+CHUNKS = tuple((sum(WIDTHS[:i]), w) for i, w in enumerate(WIDTHS))
+SHAPES = ((NK, NZX), (NZX, NK))
+HELD = tuple(min(w, SPEC - at) for at, w in CHUNKS)
 NC = len(CHUNKS)
+LOADS = 4
 GROUP = 4 * ND
+
+
+def spans(counts):
+    return tuple(zip((0,) + counts[:-1], counts))
+
+
+READY_GROUPS = spans(tuple(min((at + w) // GROUP, SPEC // GROUP) for at, w in CHUNKS))
 HALF = ND // 2
 MESH = pl.DeviceIdType.MESH
 TURN_SCALE = 2.5
@@ -42,11 +52,12 @@
 
 
 def kernel(
-    spec_ref, wind_ref, dirs_ref, fscale_ref, cg_ref, cur_ref, owner_ref, slot_ref, source_ref, mask_ref,
-    out_ref,
+    spec_hbm, wu_hbm, wv_hbm, table_hbm, cur_ref, owner_hbm, slot_hbm, source_hbm, mask_hbm,
+    out_hbm,
+    out_ref, spec_ref, wu_ref, wv_ref, table_ref, owner_ref, slot_ref, source_ref, mask_ref,
     s_ref, e_ref, hp_ref, o_ref, x1, y1, y2, z, ns_out, ns_in, ew_out, ew_in, cur_all, aux_out, aux_in,
     face_x, face_y, turn_ref, sea_ref, pick_ref,
-    p1_send, p1_recv, p2_send, p2_recv, h_send, h_recv, c_sem, a_send, a_recv,
+    p1_send, p1_recv, p2_send, p2_recv, h_send, h_recv, c_sem, a_send, a_recv, in_sem, out_sem,
 ):
     lon, lat = lax.axis_index("lon"), lax.axis_index("lat")
     n_lon, n_lat = NZX * 2, NK // 2
@@ -59,6 +70,15 @@
     def dev(lo, la):
         return {"lon": lo, "lat": la}
 
+    small = (
+        (wu_hbm, wu_ref), (wv_hbm, wv_ref), (table_hbm, table_ref), (owner_hbm, owner_ref), (slot_hbm, slot_ref),
+        (source_hbm, source_ref), (mask_hbm, mask_ref),
+    )
+    parts = [pl.ds(i * (NF // LOADS), NF // LOADS) for i in range(LOADS)]
+    loads = [pltpu.make_async_copy(spec_hbm.at[p], spec_ref.at[p], in_sem.at[i]) for i, p in enumerate(parts)]
+    loads += [pltpu.make_async_copy(a, b, in_sem.at[LOADS + i]) for i, (a, b) in enumerate(small)]
+    for load in loads:
+        load.start()
     barrier = pltpu.get_barrier_semaphore()
 
     def greet1(i, _):
@@ -79,89 +99,108 @@
     def add(f, acc):
         return acc + spec_ref[f].astype(F32)
 
-    total = lax.fori_loop(0, NF, add, jnp.zeros((ND, CELLS), F32))
+    total = jnp.zeros((ND, CELLS), F32)
+    for i in range(LOADS):
+        loads[i].wait()
+        total = lax.fori_loop(i * (NF // LOADS), (i + 1) * (NF // LOADS), add, total)
+    for load in loads[LOADS:]:
+        load.wait()
     m0 = jnp.sum(total, axis=0, keepdims=True) / SPEC
     loss0 = 0.3 * (m0 / 0.5) ** 2
-    cosd = jnp.concatenate([dirs_ref[:, :128]] * 4, axis=1)
-    sind = jnp.concatenate([dirs_ref[:, 128:]] * 4, axis=1)
-    proj = wind_ref[0:1, :] * cosd + wind_ref[1:2, :] * sind
+    across = lambda a: jnp.concatenate([a] * 4, axis=1)
+    proj = wu_ref[...] * across(table_ref[0:ND, :]) + wv_ref[...] * across(table_ref[40 : 40 + ND, :])
     s_ref[SPEC:PAD, :] = jnp.zeros((PAD - SPEC, CELLS), F32)
 
     row, col = iota((CELLS, CELLS), 0), iota((CELLS, CELLS), 1)
-    k, t = row // NZX, row % NZX
-    by_dest = onehot(col == (k // 2) * n_lon + t * 2 + k % 2)
-    regroup = onehot((row // NK == col % NZX) & (row % NK == col // NZX))
+    by_dest, regroup = [], []
+    for rows_of, columns_of in (SHAPES, SHAPES[::-1]):
+        minor, other = rows_of[1], columns_of[1]
+        major, rest = row // minor, row % minor
+        k, t = (major, rest) if minor == NZX else (rest, major)
+        by_dest.append(onehot(col == (k // 2) * n_lon + t * 2 + k % 2))
+        regroup.append(onehot((row // other == col % minor) & (row % other == col // minor)))
 
     def source(g, _):
         rows = s_ref.at[pl.ds(pl.multiple_of(g * GROUP, 16), GROUP), :]
         for i in range(4):
             f = g * 4 + i
-            drive = jnp.maximum(proj * fscale_ref[f] - 1.0, 0.0)
+            per_speed = across(table_ref[pl.ds(152 + f, 1), :])
+            rel = across(table_ref[pl.ds(192 + f, 1), :])
+            drive = jnp.maximum(proj * per_speed - 1.0, 0.0)
             gain = 0.5 * jnp.tanh(0.2 * drive)
-            rows[ND * i : ND * (i + 1), :] = spec_ref[f].astype(F32) * jnp.exp(gain - fscale_ref[NF + f] * loss0)
-        return 0
-
-    def send1(c):
+            rows[ND * i : ND * (i + 1), :] = spec_ref[f].astype(F32) * jnp.exp(gain - rel * loss0)
+        return 0
+
+    def exchange(axis, src, dst, send, recv):
+        n, mine = ((NK, me), (NZX, zx))[axis]
+
         def one(i, _):
-            k = (me + i) % NK
+            to = (mine + i) % n
             pltpu.make_async_remote_copy(
-                src_ref=x1[c].at[k], dst_ref=y1[c].at[me], send_sem=p1_send.at[c], recv_sem=p1_recv.at[c],
-                device_id=dev(zx * 2 + k % 2, k // 2), device_id_type=MESH,
+                src_ref=src.at[to], dst_ref=dst.at[mine], send_sem=send, recv_sem=recv,
+                device_id=(dev(zx * 2 + to % 2, to // 2), dev(to * 2 + core, lat))[axis], device_id_type=MESH,
             ).start()
             return 0
 
-        lax.fori_loop(1, NK, one, 0)
-        pltpu.make_async_copy(x1[c].at[me], y1[c].at[me], p1_recv.at[c]).start()
+        lax.fori_loop(1, n, one, 0)
+        pltpu.make_async_copy(src.at[mine], dst.at[mine], recv).start()
+
+    def send1(c):
+        exchange(FIRST[c], x1[c], y1[c], p1_send.at[c], p1_recv.at[c])
 
     def send2(c):
-        def one(i, _):
-            t = (zx + i) % NZX
-            pltpu.make_async_remote_copy(
-                src_ref=y2[c].at[t], dst_ref=z[c].at[zx], send_sem=p2_send.at[c], recv_sem=p2_recv.at[c],
-                device_id=dev(t * 2 + core, lat), device_id_type=MESH,
-            ).start()
-            return 0
-
-        lax.fori_loop(1, NZX, one, 0)
-        pltpu.make_async_copy(y2[c].at[zx], z[c].at[zx], p2_recv.at[c]).start()
-
-    for c, (at, width) in enumerate(CHUNKS):
-        lax.fori_loop(*SOURCE_GROUPS[c], source, 0)
+        exchange(1 - FIRST[c], y2[c], z[c], p2_send.at[c], p2_recv.at[c])
+
+    def dispatch(c):
+        at, width = CHUNKS[c]
         values = s_ref[at : at + width, :].astype(BF16)
-        x1[c][...] = dot(by_dest, values, 1, 1).astype(BF16).reshape(NK, NZX, width)
-        if c == 0:
-            pl.semaphore_wait(barrier, NK - 1 + NZX - 1 + 2)
-        send1(c)
-        if c == 0:
-            swap = pltpu.make_async_remote_copy(
-                src_ref=cur_ref, dst_ref=cur_all.at[zx, core], send_sem=c_sem.at[0], recv_sem=c_sem.at[1],
-                device_id=dev(zx * 2 + 1 - core, lat), device_id_type=MESH,
-            )
-            swap.start()
-            pltpu.make_async_copy(cur_ref, cur_all.at[zx, core], c_sem.at[1]).start()
-
-    drain(cur_all.at[zx], c_sem.at[1])
+        x1[c][...] = dot(by_dest[FIRST[c]], values, 1, 1).astype(BF16).reshape(*SHAPES[FIRST[c]], width)
+
+    def middle(c):
+        width = CHUNKS[c][1]
+        drain(y1[c], p1_recv.at[c])
+        values = dot(regroup[FIRST[c]], y1[c][...].reshape(CELLS, width), 1, 0)
+        y2[c][...] = values.astype(BF16).reshape(*SHAPES[1 - FIRST[c]], width)
+        send2(c)
 
     def share(i, _):
         t = (zx + i) % NZX
         pltpu.make_async_remote_copy(
-            src_ref=cur_all.at[zx], dst_ref=cur_all.at[zx], send_sem=c_sem.at[2], recv_sem=c_sem.at[3],
+            src_ref=cur_ref, dst_ref=cur_all.at[core, zx], send_sem=c_sem.at[0], recv_sem=c_sem.at[1],
             device_id=dev(t * 2 + core, lat), device_id_type=MESH,
         ).start()
         return 0
 
+    swap = pltpu.make_async_remote_copy(
+        src_ref=cur_all.at[core], dst_ref=cur_all.at[core], send_sem=c_sem.at[2], recv_sem=c_sem.at[3],
+        device_id=dev(zx * 2 + 1 - core, lat), device_id_type=MESH,
+    )
+
+    first_groups = -(-WIDTHS[0] // GROUP)
+    lax.fori_loop(0, first_groups, source, 0)
+    dispatch(0)
+    pl.semaphore_wait(barrier, NK - 1 + NZX - 1 + 2)
+    send1(0)
+    lax.fori_loop(first_groups, SPEC // GROUP, source, 0)
+    dispatch(2)
+    send1(2)
     lax.fori_loop(1, NZX, share, 0)
+    pltpu.make_async_copy(cur_ref, cur_all.at[core, zx], c_sem.at[1]).start()
+    dispatch(1)
+    dispatch(3)
 
     q = source_ref[...]
-    where = ((q % n_lon) // 2) * NK + (q // n_lon) * 2 + q % 2
-    where = jnp.where(mask_ref[...] > 0, where, -1)
+    from_k, from_t = (q // n_lon) * 2 + q % 2, (q % n_lon) // 2
     slots = iota((CELLS, 128), 0)
-    for y in range(4):
-        pick_ref[:, 128 * y : 128 * (y + 1)] = onehot(slots == where[y : y + 1, :])
-    both = jnp.concatenate([where, where, jnp.full((8, 128), -1, jnp.int32)], axis=0)
     edge_row = iota((16, 1), 0)
-    edge = jnp.where(edge_row < 4, both[:, 127:128], both[:, 0:1])
-    edge_pick = onehot(iota((16, CELLS), 1) == edge)
+    edge_pick = []
+    for kind, where in enumerate((from_t * NK + from_k, from_k * NZX + from_t)):
+        where = jnp.where(mask_ref[...] > 0, where, -1)
+        for y in range(4):
+            pick_ref[kind, :, 128 * y : 128 * (y + 1)] = onehot(slots == where[y : y + 1, :])
+        both = jnp.concatenate([where, where, jnp.full((8, 128), -1, jnp.int32)], axis=0)
+        edge = jnp.where(edge_row < 4, both[:, 127:128], both[:, 0:1])
+        edge_pick.append(onehot(iota((16, CELLS), 1) == edge))
     pr, pc = iota((32, CELLS), 0), iota((32, CELLS), 1)
     place = onehot(((pr < 4) & (pc == pr * 128)) | ((pr >= 20) & (pr < 24) & (pc == (pr - 20) * 128 + 127)))
 
@@ -195,19 +234,23 @@
         at, width = CHUNKS[c]
         drain(z[c], p2_recv.at[c])
         got = z[c][...].reshape(CELLS, width)
-        ew_out[c][...] = dot(edge_pick, got, 1, 0).astype(BF16)
-        energy = dot(got, pick_ref[...], 0, 0)
+        ew_out[c][...] = dot(edge_pick[FIRST[c]], got, 1, 0).astype(BF16)
+        energy = dot(got, pick_ref[FIRST[c]], 0, 0)
         for y in range(4):
             e_ref[1 + y, at : at + width, :] = energy[:, 128 * y : 128 * (y + 1)]
-        ns_out[c][0] = energy[:, :128].astype(BF16)
-        ns_out[c][1] = energy[:, 384:].astype(BF16)
+        ns_out[c][0] = energy[: HELD[c], :128].astype(BF16)
+        ns_out[c][1] = energy[: HELD[c], 384:].astype(BF16)
         for copy in halo_copies(c):
             copy.start()
 
     def send_aux():
-        drain(cur_all.at[pl.ds(0, NZX - 1)], c_sem.at[3])
-        wanted = owner_ref[...] * 16 + slot_ref[...]
-        wanted = jnp.concatenate([wanted, wanted + 8, jnp.full((8, 1), -1, jnp.int32)], axis=0)
+        swap.wait_recv()
+        owner = owner_ref[...]
+        wanted = ((owner % 2) * NZX + owner // 2) * 16 + slot_ref[...]
+        r, n = iota((16, 4), 0), iota((16, 4), 1)
+        wanted = jnp.where(r % 4 == n, wanted + 8 * (r // 4), 0).astype(F32)
+        wanted = jnp.sum(wanted, axis=1, keepdims=True).astype(jnp.int32)
+        wanted = jnp.where(iota((16, 1), 0) < 8, wanted, -1)
         blocks = onehot(iota((16, NZX * 32), 1) == wanted)
         found = dot(blocks, cur_all[...].reshape(NZX * 32, 128), 1, 0)
         sea = jnp.concatenate([jnp.zeros((8, 128), F32), mask_ref[...].astype(F32), jnp.zeros((4, 128), F32)], axis=0)
@@ -255,8 +298,8 @@
         at, width = CHUNKS[c]
         for copy in halo_copies(c):
             copy.wait_recv()
-        e_ref[0, at : at + width, :] = ns_in[c][1].astype(F32)
-        e_ref[5, at : at + width, :] = ns_in[c][0].astype(F32)
+        e_ref[0, at : at + HELD[c], :] = ns_in[c][1].astype(F32)
+        e_ref[5, at : at + HELD[c], :] = ns_in[c][0].astype(F32)
         placed = dot(ew_in[c][...].reshape(32, width), place, 0, 0)
         for y in range(4):
             hp_ref[y, at : at + width, :] = placed[:, 128 * y : 128 * (y + 1)]
@@ -266,7 +309,7 @@
     def advance(step, _):
         g, y = step // 4, step % 4
         base = g * GROUP
-        cg = cg_ref[g]
+        cg = table_ref[pl.ds(pl.multiple_of(80 + g * 8, 8), 8), :]
         fur, oxr, ful, oxl = [face_x[y, n] for n in range(4)]
         fvs, oys, fvn, oyn = face_y[y, 0], face_y[y, 1], face_y[y + 1, 0], face_y[y + 1, 1]
         sea = sea_ref[y]
@@ -303,6 +346,7 @@
     def finish(g, _):
         rows = pl.ds(pl.multiple_of(g * 4 * GROUP, 16), 4 * GROUP)
         out_ref[rows, :] = o_ref[rows, :].astype(BF16)
+        pltpu.make_async_copy(out_ref.at[rows, :], out_hbm.at[rows, :], out_sem).start()
         return 0
 
     def propagate(c):
@@ -311,83 +355,97 @@
         lax.fori_loop(first * 4, last * 4, advance, 0)
         lax.fori_loop(first, last, finish, 0)
 
-    for c, (at, width) in enumerate(CHUNKS):
-        drain(y1[c], p1_recv.at[c])
-        y2[c][...] = dot(regroup, y1[c][...].reshape(CELLS, width), 1, 0).astype(BF16).reshape(NZX, NK, width)
-        send2(c)
-        if c == 0:
-            send_aux()
-        if c == 1:
-            prepare()
-        if c >= 1:
-            pick(c - 1)
-        if c >= 2:
-            propagate(c - 2)
-    pick(NC - 1)
-    propagate(NC - 2)
-    propagate(NC - 1)
+    middle(0)
+    send1(1)
+    drain(cur_all.at[core], c_sem.at[1])
+    swap.start()
+    middle(2)
+    send1(3)
+    send_aux()
+    middle(1)
+    middle(3)
+    prepare()
+    pick(0)
+    pick(1)
+    propagate(0)
+    pick(2)
+    propagate(1)
+    pick(3)
+    propagate(2)
+    propagate(3)
 
     for c in range(NC):
-        drain(x1[c].at[pl.ds(0, NK - 1)], p1_send.at[c])
-        drain(y2[c].at[pl.ds(0, NZX - 1)], p2_send.at[c])
+        drain(x1[c].at[pl.ds(0, SHAPES[FIRST[c]][0] - 1)], p1_send.at[c])
+        drain(y2[c].at[pl.ds(0, SHAPES[1 - FIRST[c]][0] - 1)], p2_send.at[c])
         for copy in halo_copies(c):
             copy.wait_send()
-    drain(cur_ref, c_sem.at[0])
-    drain(cur_all.at[pl.ds(0, NZX - 1)], c_sem.at[2])
+    drain(cur_all.at[core, pl.ds(0, NZX - 1)], c_sem.at[0])
+    swap.wait_send()
     for copy in aux_copies():
         copy.wait_send()
+    drain(out_ref, out_sem)
 
 
 def tables():
     ratio = 1.1 ** np.arange(NF)
     theta = (np.arange(ND) + 0.5) * 2.0 * np.pi / ND
-    dirs = np.repeat(np.stack([np.cos(theta), np.sin(theta)], axis=1), 128, axis=1)
-    fscale = np.concatenate([ratio / 44.6, ratio / ratio[-1]])
-    speed = (0.53 / ratio).reshape(9, 4, 1) * np.array([1.0, -1.0]).reshape(1, 1, 2)
-    cg = np.repeat(speed.reshape(9, 8, 1), 128, axis=2)
-    return [np.asarray(a, np.float32) for a in (dirs, fscale, cg)]
+    table = np.zeros((232, 1))
+    table[0:ND, 0] = np.cos(theta)
+    table[40 : 40 + ND, 0] = np.sin(theta)
+    table[80:152, 0] = np.repeat(0.53 / ratio, 2) * np.tile([1.0, -1.0], NF)
+    table[152 : 152 + NF, 0] = ratio / 44.6
+    table[192 : 192 + NF, 0] = ratio / ratio[-1]
+    return np.repeat(table, 128, axis=1).astype(np.float32)
 
 
 def body(spec_pts, wind_u, wind_v, ocean_current, block_owner, block_slot, cell_source, land_mask):
-    vmem, smem = pl.BlockSpec(memory_space=pltpu.VMEM), pl.BlockSpec(memory_space=pltpu.SMEM)
-    dirs, fscale, cg = tables()
-    wind = jnp.stack([wind_u, wind_v])
-    per_chunk = lambda shape: [pltpu.VMEM(shape(w), BF16) for _, w in CHUNKS]
+    hbm = pl.BlockSpec(memory_space=pltpu.HBM)
+    per_chunk = lambda shape: [pltpu.VMEM(shape(i, w), BF16) for i, w in enumerate(WIDTHS)]
     dma = pltpu.SemaphoreType.DMA
     out = pl.pallas_call(
         kernel,
         out_shape=jax.ShapeDtypeStruct((SPEC * 4, 128), BF16),
-        in_specs=[vmem, vmem, vmem, smem, vmem, vmem, vmem, vmem, vmem, vmem],
-        out_specs=vmem,
+        in_specs=[hbm] * 9,
+        out_specs=hbm,
         scratch_shapes=[
+            pltpu.VMEM((SPEC * 4, 128), BF16),
+            pltpu.VMEM((NF, ND, CELLS), BF16),
+            pltpu.VMEM((1, CELLS), F32),
+            pltpu.VMEM((1, CELLS), F32),
+            pltpu.VMEM((232, 128), F32),
+            pltpu.VMEM((1, 4), jnp.int32),
+            pltpu.VMEM((1, 4), jnp.int32),
+            pltpu.VMEM((4, 128), jnp.int32),
+            pltpu.VMEM((4, 128), jnp.int32),
             pltpu.VMEM((PAD, CELLS), F32),
             pltpu.VMEM((6, PAD, 128), F32),
             pltpu.VMEM((4, PAD, 128), F32),
             pltpu.VMEM((SPEC * 4, 128), F32),
-            per_chunk(lambda w: (NK, NZX, w)),
-            per_chunk(lambda w: (NK, NZX, w)),
-            per_chunk(lambda w: (NZX, NK, w)),
-            per_chunk(lambda w: (NZX, NK, w)),
-            per_chunk(lambda w: (2, w, 128)),
-            per_chunk(lambda w: (2, w, 128)),
-            per_chunk(lambda w: (16, w)),
-            per_chunk(lambda w: (2, 16, w)),
-            pltpu.VMEM((NZX, 2, 16, 128), BF16),
+            per_chunk(lambda i, w: (*SHAPES[FIRST[i]], w)),
+            per_chunk(lambda i, w: (*SHAPES[FIRST[i]], w)),
+            per_chunk(lambda i, w: (*SHAPES[1 - FIRST[i]], w)),
+            per_chunk(lambda i, w: (*SHAPES[1 - FIRST[i]], w)),
+            per_chunk(lambda i, w: (2, HELD[i], 128)),
+            per_chunk(lambda i, w: (2, HELD[i], 128)),
+            per_chunk(lambda i, w: (16, w)),
+            per_chunk(lambda i, w: (2, 16, w)),
+            pltpu.VMEM((2, NZX, 16, 128), BF16),
             pltpu.VMEM((16, 128), BF16),
             pltpu.VMEM((4, 16, 128), BF16),
             pltpu.VMEM((4, 4, 8, 128), F32),
             pltpu.VMEM((5, 2, 8, 128), F32),
             pltpu.VMEM((4, HALF, 8, 128), F32),
             pltpu.VMEM((4, 8, 128), F32),
-            pltpu.VMEM((CELLS, CELLS), BF16),
+            pltpu.VMEM((2, CELLS, CELLS), BF16),
             dma((NC,)), dma((NC,)), dma((NC,)), dma((NC,)), dma((NC, 4)), dma((NC, 4)), dma((4,)), dma((4,)), dma((4,)),
+            dma((LOADS + 7,)), dma(()),
         ],
         compiler_params=pltpu.CompilerParams(
-            collective_id=0, has_side_effects=True, vmem_limit_bytes=48 * 2**20
+            collective_id=0, has_side_effects=True, vmem_limit_bytes=60 * 2**20
         ),
     )(
-        spec_pts, wind, jnp.asarray(dirs), jnp.asarray(fscale), jnp.asarray(cg),
-        ocean_current.reshape(16, 128), block_owner, block_slot, cell_source, land_mask,
+        spec_pts, wind_u.reshape(1, CELLS), wind_v.reshape(1, CELLS), jnp.asarray(tables()),
+        ocean_current.reshape(16, 128), block_owner.T, block_slot.T, cell_source, land_mask,
     )
     return out.reshape(NF, ND, 4, 128)
 

time: 82.2 us -> 74.2 us (0.903); the launches traced: 81 us -> 73.8 us
  local copies, waits for them, and re-layouts: 8.16 us -> 2.84 us
  Pallas kernels: 72.1 us -> 71 us
    unnamed x17 -> x1, local copies, waits for them, and re-layouts: 8.16 us -> 2.84 us
    pallas_call x1, Pallas kernels: 72.1 us -> 71 us  [body(): pl.pallas_call(kernel, out_shape=jax.ShapeDtypeStruct((SPEC * 4, 128), BF...]
where the time goes in v2:
time: 74.2 us; the launch traced here: 73.8 us
  Pallas kernels  71 us (96%)
  local copies, waits for them, and re-layouts  2.84 us (4%)
    pallas_call x1, Pallas kernels, body(): pl.pallas_call(kernel, out_shape=jax.ShapeDtypeStruct((SPEC * 4, 128), BF...  71 us
    unnamed x1, local copies, waits for them, and re-layouts  2.84 us

profile of v2, /device:TPU:1, one launch (start us, length us, event | category | flops | bytes accessed | tf_op | source)
XLA Modules:
  0.0 73.8 jit_solution(7476861878295231127)
XLA Ops:
  0.0 71.0 %shard_map.91 = bf16[5184,128]{1,0:T(8,128)(2,1)} custom-call(bf16[36,36,512]{2,1,0:T(8,128)(2,1)} %spec_hbm.1, f32[1,512]{1,0:T(1,128)} %bitcast.8, f32[1,512]{1,0:T(1,128)} %bitcast.9, f32[232,128]{1,0:T(8,128)} %constant.2.clone.table_hbm, bf16[16,128]{1,0:T(8,128)(2,1)} %bitcast.7, s32[1,4]{1,0:T(1,128)} %bitcast.10, s32[1,4]{1,0:T(1,128)} %bitcast.11, ...), custom_call_target="tpu_custom_call" | custom-call | tf_op jit(solution)/shard_map/pallas_call | solution.py:405
  71.0 2.8 %copy.11 = bf16[36,36,4,128]{3,2,1,0:T(4,128)(2,1)} copy(bf16[36,36,4,128]{3,2,1,0:T(4,128)(2,1)} %bitcast.6) | data formatting | bytes 2654208

commit v3 on v2

--- a/solution.py
+++ b/solution.py
@@ -14,7 +14,7 @@
 PAD = 1408
 CELLS = 512
 NK, NZX = 16, 32
-WIDTHS = (512, 128, 640, 128)
+WIDTHS = (384, 384, 512, 128)
 FIRST = (0, 0, 1, 1)
 CHUNKS = tuple((sum(WIDTHS[:i]), w) for i, w in enumerate(WIDTHS))
 SHAPES = ((NK, NZX), (NZX, NK))
@@ -53,11 +53,11 @@
 
 def kernel(
     spec_hbm, wu_hbm, wv_hbm, table_hbm, cur_ref, owner_hbm, slot_hbm, source_hbm, mask_hbm,
-    out_hbm,
-    out_ref, spec_ref, wu_ref, wv_ref, table_ref, owner_ref, slot_ref, source_ref, mask_ref,
+    out_ref,
+    spec_ref, wu_ref, wv_ref, table_ref, owner_ref, slot_ref, source_ref, mask_ref,
     s_ref, e_ref, hp_ref, o_ref, x1, y1, y2, z, ns_out, ns_in, ew_out, ew_in, cur_all, aux_out, aux_in,
     face_x, face_y, turn_ref, sea_ref, pick_ref,
-    p1_send, p1_recv, p2_send, p2_recv, h_send, h_recv, c_sem, a_send, a_recv, in_sem, out_sem,
+    p1_send, p1_recv, p2_send, p2_recv, h_send, h_recv, c_sem, a_send, a_recv, in_sem,
 ):
     lon, lat = lax.axis_index("lon"), lax.axis_index("lat")
     n_lon, n_lat = NZX * 2, NK // 2
@@ -346,7 +346,6 @@
     def finish(g, _):
         rows = pl.ds(pl.multiple_of(g * 4 * GROUP, 16), 4 * GROUP)
         out_ref[rows, :] = o_ref[rows, :].astype(BF16)
-        pltpu.make_async_copy(out_ref.at[rows, :], out_hbm.at[rows, :], out_sem).start()
         return 0
 
     def propagate(c):
@@ -383,7 +382,6 @@
     swap.wait_send()
     for copy in aux_copies():
         copy.wait_send()
-    drain(out_ref, out_sem)
 
 
 def tables():
@@ -406,9 +404,8 @@
         kernel,
         out_shape=jax.ShapeDtypeStruct((SPEC * 4, 128), BF16),
         in_specs=[hbm] * 9,
-        out_specs=hbm,
+        out_specs=pl.BlockSpec(memory_space=pltpu.VMEM),
         scratch_shapes=[
-            pltpu.VMEM((SPEC * 4, 128), BF16),
             pltpu.VMEM((NF, ND, CELLS), BF16),
             pltpu.VMEM((1, CELLS), F32),
             pltpu.VMEM((1, CELLS), F32),
@@ -438,15 +435,18 @@
             pltpu.VMEM((4, 8, 128), F32),
             pltpu.VMEM((2, CELLS, CELLS), BF16),
             dma((NC,)), dma((NC,)), dma((NC,)), dma((NC,)), dma((NC, 4)), dma((NC, 4)), dma((4,)), dma((4,)), dma((4,)),
-            dma((LOADS + 7,)), dma(()),
+            dma((LOADS + 7,)),
         ],
         compiler_params=pltpu.CompilerParams(
-            collective_id=0, has_side_effects=True, vmem_limit_bytes=60 * 2**20
+            collective_id=0, has_side_effects=True, vmem_limit_bytes=50 * 2**20
         ),
-    )(
-        spec_pts, wind_u.reshape(1, CELLS), wind_v.reshape(1, CELLS), jnp.asarray(tables()),
-        ocean_current.reshape(16, 128), block_owner.T, block_slot.T, cell_source, land_mask,
-    )
+    )(*[
+        pltpu.with_memory_space_constraint(a, pltpu.HBM)
+        for a in (
+            spec_pts, wind_u.reshape(1, CELLS), wind_v.reshape(1, CELLS), jnp.asarray(tables()),
+            ocean_current.reshape(16, 128), block_owner.T, block_slot.T, cell_source, land_mask,
+        )
+    ])
     return out.reshape(NF, ND, 4, 128)
 
 

time: 74.2 us -> 66.4 us (0.89)
  Pallas kernels: 71 us -> 65.2 us
  local copies, waits for them, and re-layouts: 2.84 us -> 1.06 us
    pallas_call x1, Pallas kernels: 71 us -> 65.2 us  [body(): pl.pallas_call(kernel, out_shape=jax.ShapeDtypeStruct((SPEC * 4, 128), BF...]
    unnamed x1, local copies, waits for them, and re-layouts: 2.84 us -> 1.06 us
where the time goes in v3:
time: 66.4 us; the launch traced here: 66.2 us
  Pallas kernels  65.2 us (98%)
  local copies, waits for them, and re-layouts  1.06 us (2%)
    pallas_call x1, Pallas kernels, body(): pl.pallas_call(kernel, out_shape=jax.ShapeDtypeStruct((SPEC * 4, 128), BF...  65.2 us

profile of v3, /device:TPU:1, one launch (start us, length us, event | category | flops | bytes accessed | tf_op | source)
XLA Modules:
  0.0 66.2 jit_solution(10514916722652537097)
XLA Ops:
  0.0 65.2 %shard_map.91 = bf16[5184,128]{1,0:T(8,128)(2,1)S(1)} custom-call(bf16[36,36,512]{2,1,0:T(8,128)(2,1)} %spec_hbm.1, f32[1,512]{1,0:T(1,128)} %bitcast.8, f32[1,512]{1,0:T(1,128)} %bitcast.9, f32[232,128]{1,0:T(8,128)} %constant.2.clone.table_hbm, bf16[16,128]{1,0:T(8,128)(2,1)} %bitcast.7, s32[1,4]{1,0:T(1,128)} %bitcast.10, s32[1,4]{1,0:T(1,128)} %bitcast.11, ...), custom_call_target="tpu_custom_call" | custom-call | tf_op jit(solution)/shard_map/pallas_call | solution.py:403
  65.2 1.1 %copy.11 = bf16[36,36,4,128]{3,2,1,0:T(4,128)(2,1)} copy(bf16[36,36,4,128]{3,2,1,0:T(4,128)(2,1)S(1)} %bitcast.6) | data formatting | bytes 2654208

commit v4 on v3

--- a/solution.py
+++ b/solution.py
@@ -15,7 +15,7 @@
 CELLS = 512
 NK, NZX = 16, 32
 WIDTHS = (384, 384, 512, 128)
-FIRST = (0, 0, 1, 1)
+FIRST = (1, 1, 0, 0)
 CHUNKS = tuple((sum(WIDTHS[:i]), w) for i, w in enumerate(WIDTHS))
 SHAPES = ((NK, NZX), (NZX, NK))
 HELD = tuple(min(w, SPEC - at) for at, w in CHUNKS)

time: 66.4 us -> 66 us (level)
  no operation moved by 1% of the time
where the time goes in v4:
time: 66 us; the launch traced here: 65.8 us
  Pallas kernels  64.8 us (98%)
  local copies, waits for them, and re-layouts  1.06 us (2%)
    pallas_call x1, Pallas kernels, body(): pl.pallas_call(kernel, out_shape=jax.ShapeDtypeStruct((SPEC * 4, 128), BF...  64.8 us

profile of v4, /device:TPU:1, one launch (start us, length us, event | category | flops | bytes accessed | tf_op | source)
XLA Modules:
  0.0 65.8 jit_solution(5047238646870950738)
XLA Ops:
  0.0 64.8 %shard_map.91 = bf16[5184,128]{1,0:T(8,128)(2,1)S(1)} custom-call(bf16[36,36,512]{2,1,0:T(8,128)(2,1)} %spec_hbm.1, f32[1,512]{1,0:T(1,128)} %bitcast.8, f32[1,512]{1,0:T(1,128)} %bitcast.9, f32[232,128]{1,0:T(8,128)} %constant.2.clone.table_hbm, bf16[16,128]{1,0:T(8,128)(2,1)} %bitcast.7, s32[1,4]{1,0:T(1,128)} %bitcast.10, s32[1,4]{1,0:T(1,128)} %bitcast.11, ...), custom_call_target="tpu_custom_call" | custom-call | tf_op jit(solution)/shard_map/pallas_call | solution.py:403
  64.8 1.1 %copy.11 = bf16[36,36,4,128]{3,2,1,0:T(4,128)(2,1)} copy(bf16[36,36,4,128]{3,2,1,0:T(4,128)(2,1)S(1)} %bitcast.6) | data formatting | bytes 2654208

commit v5 on v4

--- a/solution.py
+++ b/solution.py
@@ -368,8 +368,8 @@
     pick(1)
     propagate(0)
     pick(2)
+    pick(3)
     propagate(1)
-    pick(3)
     propagate(2)
     propagate(3)
 

time: 66 us -> 64.3 us (0.974)
  the two profiles are of different devices: /device:TPU:1 before, /device:TPU:24 now
where the time goes in v5:
time: 64.3 us; the launch traced here: 64.2 us
  Pallas kernels  63.1 us (98%)
  local copies, waits for them, and re-layouts  1.06 us (2%)
    pallas_call x1, Pallas kernels, body(): pl.pallas_call(kernel, out_shape=jax.ShapeDtypeStruct((SPEC * 4, 128), BF...  63.1 us

profile of v5, /device:TPU:24, one launch (start us, length us, event | category | flops | bytes accessed | tf_op | source)
XLA Modules:
  0.0 64.2 jit_solution(13754912585843737224)
XLA Ops:
  0.0 63.1 %shard_map.91 = bf16[5184,128]{1,0:T(8,128)(2,1)S(1)} custom-call(bf16[36,36,512]{2,1,0:T(8,128)(2,1)} %spec_hbm.1, f32[1,512]{1,0:T(1,128)} %bitcast.8, f32[1,512]{1,0:T(1,128)} %bitcast.9, f32[232,128]{1,0:T(8,128)} %constant.2.clone.table_hbm, bf16[16,128]{1,0:T(8,128)(2,1)} %bitcast.7, s32[1,4]{1,0:T(1,128)} %bitcast.10, s32[1,4]{1,0:T(1,128)} %bitcast.11, ...), custom_call_target="tpu_custom_call" | custom-call | tf_op jit(solution)/shard_map/pallas_call | solution.py:403
  63.1 1.1 %copy.11 = bf16[36,36,4,128]{3,2,1,0:T(4,128)(2,1)} copy(bf16[36,36,4,128]{3,2,1,0:T(4,128)(2,1)S(1)} %bitcast.6) | data formatting | bytes 2654208
